TPU v7x, 128 devices: a whole 4x4x4 slice. The times are simulated.
128 devices in a mesh: dp: 16 (over z, x_lo, core), mp: 8 (over x_hi, y).
Axes of the slice: x: 4 (x_hi: 2, x_lo: 2; x = x_hi * 2 + x_lo), y: 4, z: 4, core: 2. Of those that a mesh axis runs over, the one named last changes fastest.
Arguments:
- tokens: bfloat16 [8192, 3072], P('dp', 'mp'), may hold values from -180 to 180
- update_grad: bfloat16 [8192, 3072], P('dp', 'mp'), may hold values from -1 to 1
- weight_in: bfloat16 [3072, 9216], P('dp', 'mp'), may hold values from -0.109375 to 0.109375
- weight_out: bfloat16 [3072, 3072], P('dp', 'mp'), may hold values from -0.875 to 0.875
Outputs:
- update: bfloat16 [8192, 3072], P('dp', 'mp')
- input_grad: bfloat16 [8192, 3072], P('dp', 'mp')
- weight_in_grad: float32 [3072, 9216], P('dp', 'mp')
- weight_out_grad: float32 [3072, 3072], P('dp', 'mp')
All inputs are finite; a program needn't handle non-finite values.
Results may differ from a plain program's by a relative error of at most 0.023.
Values may be sent and summed in bfloat16 or wider, within the bound.
No kernel may reach another device: no remote copies, remote signals or barrier semaphores. Data moves between devices by JAX's collectives and lax.ppermute only.
A program may use at most 128 MiB of HBM per device.

v0:
```python
import jax
import jax.numpy as jnp
from jax import lax
from jax.sharding import PartitionSpec as P

HD = 128
PATCH = 256


epsilon = 1e-06


def norm_rows(vector):
    centred = vector - jnp.mean(vector, axis=-1, keepdims=True)
    inverse = lax.rsqrt(jnp.mean(centred * centred, axis=-1, keepdims=True) + epsilon)
    return (centred * inverse, inverse)


def norm_back(incoming, normed, inverse):
    mean_in = jnp.mean(incoming, axis=-1, keepdims=True)
    mean_cross = jnp.mean(incoming * normed, axis=-1, keepdims=True)
    return inverse * (incoming - mean_in - normed * mean_cross)


def attend_forward(projected):
    wide = jnp.float32
    query_norm, query_scale = norm_rows(projected[:, :, :, 0])
    key_norm, key_scale = norm_rows(projected[:, :, :, 1])
    query_low = query_norm.astype(jnp.bfloat16)
    key_low = key_norm.astype(jnp.bfloat16)
    value_low = projected[:, :, :, 2].astype(jnp.bfloat16)
    scores = jnp.einsum(
        "bphe,bqhe->bhpq", query_low, key_low, preferred_element_type=wide
    ) * HD ** (-0.5)
    expo = jnp.exp(scores)
    attention = expo / jnp.sum(expo, axis=-1, keepdims=True)
    rounded = attention.astype(jnp.bfloat16)
    head_out = jnp.einsum(
        "bhpq,bqhe->bphe", rounded, value_low, preferred_element_type=wide
    ).astype(jnp.bfloat16)
    saved = (
        attention,
        rounded,
        query_low,
        key_low,
        value_low,
        query_norm,
        query_scale,
        key_norm,
        key_scale,
    )
    return (head_out, saved)


def attend_backward(incoming, saved):
    wide = jnp.float32
    (
        attention,
        rounded,
        query_low,
        key_low,
        value_low,
        query_norm,
        query_scale,
        key_norm,
        key_scale,
    ) = saved
    mixing_grad = jnp.einsum("bphe,bqhe->bhpq", incoming, value_low, preferred_element_type=wide)
    score_grad = attention * (
        mixing_grad - jnp.sum(mixing_grad * attention, axis=-1, keepdims=True)
    )
    score_low = (score_grad * HD ** (-0.5)).astype(jnp.bfloat16)
    value_grad = jnp.einsum("bhpq,bphe->bqhe", rounded, incoming, preferred_element_type=wide)
    query_grad = jnp.einsum("bhpq,bqhe->bphe", score_low, key_low, preferred_element_type=wide)
    key_grad = jnp.einsum("bhpq,bphe->bqhe", score_low, query_low, preferred_element_type=wide)
    query_grad = norm_back(query_grad, query_norm, query_scale)
    key_grad = norm_back(key_grad, key_norm, key_scale)
    return jnp.stack([query_grad, key_grad, value_grad], axis=3).astype(jnp.bfloat16)


def local(tokens, update_grad, weight_in, weight_out):
    all_tokens, all_update_grad = (
        lax.all_gather(tokens, "mp", axis=1, tiled=True),
        lax.all_gather(update_grad, "mp", axis=1, tiled=True),
    )
    whole_in, whole_out = (
        lax.all_gather(weight_in, "dp", axis=0, tiled=True),
        lax.all_gather(weight_out, "dp", axis=0, tiled=True),
    )
    normed, inv_tokens = norm_rows(all_tokens.astype(jnp.float32))
    normed_low = normed.astype(jnp.bfloat16)
    projected = jnp.dot(normed_low, whole_in, preferred_element_type=jnp.float32)
    attend_grad = jnp.dot(all_update_grad, whole_out, preferred_element_type=jnp.float32).astype(
        jnp.bfloat16
    )
    token_rows = projected.shape[0]
    images_here = token_rows // PATCH
    heads_here = whole_out.shape[1] // HD
    head_out, saved = attend_forward(projected.reshape(images_here, PATCH, heads_here, 3, HD))
    attended = head_out.reshape(token_rows, heads_here * HD)
    partial_value = jnp.einsum("ta,da->td", attended, whole_out, preferred_element_type=jnp.float32)
    update = lax.psum_scatter(
        partial_value.astype(jnp.bfloat16), "mp", scatter_dimension=1, tiled=True
    )
    head_grad_in = attend_grad.reshape(images_here, PATCH, heads_here, HD)
    projected_grad = attend_backward(head_grad_in, saved).reshape(token_rows, -1)
    merged_part = jnp.einsum(
        "td,tc->dc", normed_low, projected_grad, preferred_element_type=jnp.float32
    )
    joined = lax.psum_scatter(
        jnp.concatenate(
            [
                merged_part,
                jnp.einsum(
                    "td,ta->da", all_update_grad, attended, preferred_element_type=jnp.float32
                ),
            ],
            axis=1,
        ).astype(jnp.bfloat16),
        "dp",
        scatter_dimension=0,
        tiled=True,
    ).astype(jnp.float32)
    merged_width = projected_grad.shape[1]
    weight_in_grad = joined[:, :merged_width]
    weight_out_grad = joined[:, merged_width:]
    normed_grad = jnp.einsum(
        "tc,dc->td", projected_grad, whole_in, preferred_element_type=jnp.float32
    )
    own_width = tokens.shape[1]
    first_column = lax.axis_index("mp") * own_width
    summed = lax.psum(normed_grad.astype(jnp.bfloat16), "mp").astype(jnp.float32)
    input_grad = lax.dynamic_slice_in_dim(
        norm_back(summed, normed, inv_tokens), first_column, own_width, 1
    )
    return (update, input_grad.astype(jnp.bfloat16), weight_in_grad, weight_out_grad)


def solution(mesh):
    return jax.shard_map(
        local,
        mesh=mesh,
        in_specs=(P("dp", "mp"), P("dp", "mp"), P("dp", "mp"), P("dp", "mp")),
        out_specs=(P("dp", "mp"), P("dp", "mp"), P("dp", "mp"), P("dp", "mp")),
        check_vma=False,
    )
```

profile of v0, /device:TPU:0, one launch (start us, length us, event | category | flops | bytes accessed | tf_op | source)
XLA Modules:
  0.0 580.2 jit_solution(1780934254076994369)
XLA Ops:
  10.0 36.7 %all-gather.9.cloned.1.call-done = bf16[3072,384]{1,0:T(8,128)(2,1)} async-done(((bf16[192,384]{1,0:T(8,128)(2,1)}), bf16[3072,384]{1,0:T(8,128)(2,1)}) %all-gather.9.cloned.1.call-update) | async-done | bytes 2359312 | tf_op jit(solution)/shard_map/all_gather | solution.py:88
  46.7 66.0 %all-gather.11.cloned.1.call-done = bf16[512,3072]{1,0:T(8,128)(2,1)} async-done(((bf16[512,384]{1,0:T(8,128)(2,1)}), bf16[512,3072]{1,0:T(8,128)(2,1)}) %all-gather.11.cloned.1.call-update) | async-done | bytes 3145744 | tf_op jit(solution)/shard_map/all_gather | solution.py:84
  112.7 4.4 convolution_convert_fusion.5
  117.5 59.2 %all-gather.5.cloned.1.call-done = bf16[512,3072]{1,0:T(8,128)(2,1)} async-done(((bf16[512,384]{1,0:T(8,128)(2,1)}), bf16[512,3072]{1,0:T(8,128)(2,1)}) %all-gather.5.cloned.1.call-update) | async-done | bytes 3145744 | tf_op jit(solution)/shard_map/all_gather | solution.py:83
  176.7 2.5 convert_reduce_fusion
  180.5 41.7 %all-gather.7.cloned.1.call-done = bf16[3072,1152]{1,0:T(8,128)(2,1)} async-done(((bf16[192,1152]{1,0:T(8,128)(2,1)}), bf16[3072,1152]{1,0:T(8,128)(2,1)}) %all-gather.7.cloned.1.call-update) | async-done | bytes 7077904 | tf_op jit(solution)/shard_map/all_gather | solution.py:87
  222.2 8.4 %fusion.9 = f32[512,1152]{0,1:T(8,128)} fusion(bf16[3072,1152]{1,0:T(8,128)(2,1)} %all-gather.7.cloned.1.call-done, bf16[512,3072]{1,0:T(8,128)(2,1)S(1)} %copy-done, f32[512]{0:T(512)S(1)} %add_rsqrt_fusion.2, f32[512]{0:T(512)S(1)} %broadcast_multiply_fusion.8), kind=kOutput, calls=%fused_computation.19 | convolution fusion | flops 3630170112 | bytes 12587008 | tf_op jit(solution)/shard_map/dot_general | solution.py:92
  230.6 4.1 reshape.83
  234.7 1.9 fusion.56
  236.7 2.7 slice.21
  241.0 3.1 fusion.29
  244.1 2.5 fusion.24
  246.6 2.7 fusion.41
  249.3 5.4 fusion.55
  254.7 5.4 fusion.54
  262.9 1.6 fusion.37
  264.5 1.6 fusion.36
  268.7 8.8 %convolution_convert_fusion.1 = bf16[512,3072]{1,0:T(8,128)(2,1)} fusion(bf16[512,1152]{0,1:T(8,128)(2,1)S(1)} %bitcast.90, bf16[3072,1152]{1,0:T(8,128)(2,1)} %all-gather.7.cloned.1.call-done), kind=kOutput, calls=%fused_computation.9 | convolution fusion | flops 3625451520 | bytes 11403264 | tf_op jit(solution)/shard_map/tc,dc->td/dot_general | solution.py:127
  278.5 1.8 fusion.23
  280.8 3.5 convolution_convert_fusion.2
  284.3 4.9 copy.66
  289.5 3.4 fusion.4
  292.9 4.3 convolution_convert_fusion
  297.3 9.8 %pad_maximum_fusion = bf16[3072,1536]{0,1:T(8,128)(2,1)} fusion(bf16[3072,384]{0,1:T(8,128)(2,1)S(1)} %fusion.4, bf16[3072,1152]{0,1:T(8,128)(2,1)S(1)} %convolution_convert_fusion), kind=kLoop, calls=%fused_computation.2 | loop fusion | flops 18874368 | bytes 18874368 | tf_op jit(solution)/shard_map/concatenate | solution.py:111
  307.1 12.7 %copy.68 = bf16[3072,1536]{1,0:T(8,128)(2,1)} copy(bf16[3072,1536]{0,1:T(8,128)(2,1)} %pad_maximum_fusion) | data formatting | bytes 18874368
  319.9 58.1 %all-reduce.2.cloned.1.call-done = bf16[512,3072]{1,0:T(8,128)(2,1)} async-done(((bf16[512,3072]{1,0:T(8,128)(2,1)}), bf16[512,3072]{1,0:T(8,128)(2,1)}) %all-reduce.2.cloned.1.call-update) | async-done | bytes 3145744 | tf_op jit(solution)/shard_map/psum | solution.py:132
  378.0 2.8 convert_element_type.65
  380.8 2.3 convert_reduce_fusion.1
  384.2 75.5 %reduce-scatter.7.cloned.1.call-done = bf16[384,512]{1,0:T(8,128)(2,1)} async-done(((bf16[3072,512]{1,0:T(8,128)(2,1)}), bf16[384,512]{1,0:T(8,128)(2,1)}) %reduce-scatter.7.cloned.1.call-update) | async-done | bytes 393232
  459.7 1.9 copy.67
  461.6 107.9 %reduce-scatter.9.cloned.1.call-done = bf16[192,1536]{1,0:T(8,128)(2,1)} async-done(((bf16[3072,1536]{1,0:T(8,128)(2,1)}), bf16[192,1536]{1,0:T(8,128)(2,1)}) %reduce-scatter.9.cloned.1.call-update) | async-done | bytes 589840
  571.0 1.3 copy.56
  (71 shorter events, 16.8 us)
Async XLA Ops:
  7.2 39.6 %all-gather.9.cloned.1.call-start = ((), (), s32[]{:S(2)}) async-start(), calls=%async_computation.4 | async-start | bytes 2506752 | tf_op jit(solution)/shard_map/all_gather | solution.py:88
  7.9 104.8 %all-gather.11.cloned.1.call-start = ((), (), s32[]{:S(2)}) async-start(), calls=%async_computation.5 | async-start | bytes 3538944 | tf_op jit(solution)/shard_map/all_gather | solution.py:84
  8.6 168.0 %all-gather.5.cloned.1.call-start = ((), (), s32[]{:S(2)}) async-start(), calls=%async_computation.2 | async-start | bytes 3538944 | tf_op jit(solution)/shard_map/all_gather | solution.py:83
  9.4 212.8 %all-gather.7.cloned.1.call-start = ((), (), s32[]{:S(2)}) async-start(), calls=%async_computation.3 | async-start | bytes 7520256 | tf_op jit(solution)/shard_map/all_gather | solution.py:87
  10.0 368.0 %all-reduce.2.cloned.1.call-start = ((), (), s32[]{:S(2)}) async-start(), calls=%async_computation.6 | async-start | bytes 6291456 | tf_op jit(solution)/shard_map/psum | solution.py:132
  176.7 2.8 copy-start
  179.5 51.1 %copy-start.11 = (f32[512]{0:T(512)}, f32[512]{0:T(512)S(1)}, u32[]{:S(2)}) copy-start(f32[512]{0:T(512)S(1)} %broadcast_multiply_fusion.8) | copy-start | bytes 6148
  180.5 50.1 %copy-start.9 = (f32[512]{0:T(512)}, f32[512]{0:T(512)S(1)}, u32[]{:S(2)}) copy-start(f32[512]{0:T(512)S(1)} %add_rsqrt_fusion.2) | copy-start | bytes 6148
  236.7 2.9 copy-start.1
  236.7 3.1 copy-start.2
  254.7 11.3 %copy-start.6 = (bf16[2,256,3,1,128]{1,4,2,0,3:T(8,128)(2,1)S(1)}, bf16[2,256,3,1,128]{1,4,2,0,3:T(8,128)(2,1)}, u32[]{:S(2)}) copy-start(bf16[2,256,3,1,128]{1,4,2,0,3:T(8,128)(2,1)} %fusion.24) | copy-start | bytes 1179652
  267.7 1.1 copy-start.7
  277.5 1.0 copy-start.4
  277.5 182.1 %reduce-scatter.7.cloned.1.call-start = ((), (), s32[]{:S(2)}) async-start(), calls=%async_computation.7 | async-start | bytes 3538944
  278.5 2.3 copy-start.13
  289.2 3.7 copy-start.10
  289.2 3.7 copy-start.12
  289.2 280.2 %reduce-scatter.9.cloned.1.call-start = ((), (), s32[]{:S(2)}) async-start(), calls=%async_computation.8 | async-start | bytes 10027008
  289.5 3.4 copy-start.8
  377.9 2.8 copy-start.3
  569.5 2.8 copy-start.5
Sparse Core Ops, SparseCore 0:
  9.7 36.9 all-gather.8
  48.9 63.7 all-gather.10
  114.9 61.7 all-gather.4
  178.3 43.9 all-gather.6
  277.6 100.2 all-reduce.1
  381.6 77.9 reduce-scatter.6
  462.1 107.3 reduce-scatter.8
where the time goes:
time: 581 us; the launch traced here: 580 us
  waiting for transfers between devices  448 us (77%)
  matrix products  53.8 us (9%)
  local copies, waits for them, and re-layouts  36.7 us (6%)
  other arithmetic  27.1 us (5%)
  between operations  14.4 us (2%)
    unnamed x9, waiting for transfers between devices  186 us
    all_gather x1, waiting for transfers between devices, local(): lax.all_gather(update_grad, 'mp', axis=1, tiled=True)  66 us
    all_gather x1, waiting for transfers between devices, local(): lax.all_gather(tokens, 'mp', axis=1, tiled=True)  59.2 us
    psum x1, waiting for transfers between devices, local(): lax.psum(normed_grad.astype(jnp.bfloat16), 'mp').astype(jnp.float32)  58.1 us
    all_gather x1, waiting for transfers between devices, local(): lax.all_gather(weight_in, 'dp', axis=0, tiled=True)  41.7 us
    all_gather x1, waiting for transfers between devices, local(): lax.all_gather(weight_out, 'dp', axis=0, tiled=True)  36.7 us
    unnamed x37, local copies, waits for them, and re-layouts  24.8 us
  transfers between devices with their start and end apart: 7, of which 7 were waited for; matrix products, arithmetic and copies ran while one was open for 10% of the time, Pallas kernels for 0%

commit v1 on v0

v1 whole, which is shorter than its diff:
```python
import functools

import jax
import jax.numpy as jnp
from jax import lax
from jax.experimental import pallas as pl
from jax.experimental.pallas import tpu as pltpu
from jax.sharding import PartitionSpec as P

F32 = jnp.float32
BF16 = jnp.bfloat16

D = 3072
HD = 128
PATCH = 256
TOK = 512
HEADS = 3
WQ = HEADS * 3 * HD
WA = HEADS * HD
WALL = WQ + WA
FEAT = 384
ROWS = 192
EPS = 1e-06
EXTRA = 32
VMEM = 56 * 1024 * 1024

NN = (((1,), (0,)), ((), ()))
NT = (((1,), (1,)), ((), ()))
TN = (((0,), (0,)), ((), ()))

PIECES = ((0, 0), (0, 3), (0, 1), (0, 2), (1, 0), (1, 3), (1, 1), (1, 2))
BLOCKS = ((1, 2), (0, 2), (1, 1), (1, 3), (0, 1), (0, 3), (1, 0), (0, 0))


def dot(a, b, dims):
    return lax.dot_general(a, b, dims, preferred_element_type=F32)


def mp_perm(dx, dy):
    return [(x * 4 + y, ((x + dx) % 2) * 4 + (y + dy) % 4) for x in range(2) for y in range(4)]


def dp_perm(dz, dx, dc):
    return [
        ((z * 2 + x) * 2 + c, (((z + dz) % 4) * 2 + (x + dx) % 2) * 2 + (c + dc) % 2)
        for z in range(4)
        for x in range(2)
        for c in range(2)
    ]


def y_up(v):
    return lax.ppermute(v, "mp", mp_perm(0, 1))


def y_down(v):
    return lax.ppermute(v, "mp", mp_perm(0, 3))


def x_far(v):
    return lax.ppermute(v, "mp", mp_perm(1, 0))


def z_up(v):
    return lax.ppermute(v, "dp", dp_perm(1, 0, 0))


def z_down(v):
    return lax.ppermute(v, "dp", dp_perm(3, 0, 0))


def x_near(v):
    return lax.ppermute(v, "dp", dp_perm(0, 1, 0))


def other_core(v):
    return lax.ppermute(v, "dp", dp_perm(0, 0, 1))


def params():
    return pltpu.CompilerParams(vmem_limit_bytes=VMEM)


def cost(flops, nbytes):
    return pl.CostEstimate(flops=flops, bytes_accessed=nbytes, transcendentals=0)


def whole(shape):
    return pl.BlockSpec(shape, lambda *_: (0,) * len(shape))


def norm_rows(v):
    centred = v - jnp.mean(v, axis=-1, keepdims=True)
    inverse = lax.rsqrt(jnp.mean(centred * centred, axis=-1, keepdims=True) + EPS)
    return centred * inverse, inverse


def norm_back(incoming, normed, inverse):
    mean_in = jnp.mean(incoming, axis=-1, keepdims=True)
    mean_cross = jnp.mean(incoming * normed, axis=-1, keepdims=True)
    return inverse * (incoming - mean_in - normed * mean_cross)


PREP = 128


def prep_kernel(place, own, ap, am, fat, fag, xx, bp, bm, fbt, fbg, low, grad, low_t, grad_t, mean, inv):
    t_refs = [own.at[0], ap.at[0], am.at[0], fat, xx.at[0], bp.at[0], bm.at[0], fbt]
    g_refs = [own.at[1], ap.at[1], am.at[1], fag, xx.at[1], bp.at[1], bm.at[1], fbg]
    total = jnp.zeros((PREP, FEAT), F32)
    for r in t_refs:
        total = total + r[...].astype(F32)
    m = jnp.sum(total, axis=-1, keepdims=True) * (1.0 / D)
    total = jnp.zeros((PREP, FEAT), F32)
    for r in t_refs:
        c = r[...].astype(F32) - m
        total = total + c * c
    i = lax.rsqrt(jnp.sum(total, axis=-1, keepdims=True) * (1.0 / D) + EPS)
    mean[...] = m
    inv[...] = i
    for k in range(8):
        at = pl.multiple_of(place[k] * FEAT, FEAT)
        n = ((t_refs[k][...].astype(F32) - m) * i).astype(BF16)
        low[:, pl.ds(at, FEAT)] = n
        low_t[pl.ds(at, FEAT), :] = n.T
        g = g_refs[k][...]
        grad[:, pl.ds(at, FEAT)] = g
        grad_t[pl.ds(at, FEAT), :] = g.T


def prep(place, pieces):
    pair = pl.BlockSpec((2, PREP, FEAT), lambda i, s: (0, i, 0))
    one = pl.BlockSpec((PREP, FEAT), lambda i, s: (i, 0))
    row = pl.BlockSpec((PREP, D), lambda i, s: (i, 0))
    col = pl.BlockSpec((D, PREP), lambda i, s: (0, i))
    stat = pl.BlockSpec((PREP, 1), lambda i, s: (i, 0))
    return pl.pallas_call(
        prep_kernel,
        grid_spec=pltpu.PrefetchScalarGridSpec(
            num_scalar_prefetch=1,
            grid=(TOK // PREP,),
            in_specs=[pair, pair, pair, one, one, pair, pair, pair, one, one],
            out_specs=[row, row, col, col, stat, stat],
        ),
        out_shape=[
            jax.ShapeDtypeStruct((TOK, D), BF16),
            jax.ShapeDtypeStruct((TOK, D), BF16),
            jax.ShapeDtypeStruct((D, TOK), BF16),
            jax.ShapeDtypeStruct((D, TOK), BF16),
            jax.ShapeDtypeStruct((TOK, 1), F32),
            jax.ShapeDtypeStruct((TOK, 1), F32),
        ],
        compiler_params=params(),
        cost_estimate=cost(20 * TOK * D, 6 * TOK * D * 2),
        name="prep",
    )(place, *pieces)


def eye():
    return lax.broadcasted_iota(jnp.int32, (HD, HD), 0) == lax.broadcasted_iota(jnp.int32, (HD, HD), 1)


def attend_kernel(low, grad, w, attended, dproj, stats, acc, gacc, wsum, rows):
    k = pl.program_id(0)

    @pl.when(k == 0)
    def _():
        acc[...] = jnp.zeros_like(acc)
        gacc[...] = jnp.zeros_like(gacc)
        wsum[...] = jnp.zeros_like(wsum)
        rows[...] = jnp.zeros_like(rows)

    acc[...] += dot(low[...], w[:, :WQ], NN)
    gacc[...] += dot(grad[...], w[:, WQ:], NN)
    wsum[...] += jnp.sum(w[:, :WQ].astype(F32), axis=0, keepdims=True)

    @pl.when(k == 7)
    def _():
        scale = HD**-0.5
        for b in range(TOK // PATCH):
            at = slice(b * PATCH, (b + 1) * PATCH)
            sum_in = jnp.zeros((PATCH, HD), F32)
            sum_cross = jnp.zeros((PATCH, HD), F32)
            for h in range(HEADS):
                c = h * 3 * HD
                parts = [slice(c + p * HD, c + (p + 1) * HD) for p in range(3)]
                q, key, v = [acc[at, s] for s in parts]
                qn, qs = norm_rows(q)
                kn, ks = norm_rows(key)
                ql, kl, vl = qn.astype(BF16), kn.astype(BF16), v.astype(BF16)
                expo = jnp.exp(dot(ql, kl, NT) * scale)
                att = expo / jnp.sum(expo, axis=-1, keepdims=True)
                att_low = att.astype(BF16)
                hs = slice(h * HD, (h + 1) * HD)
                attended[at, hs] = dot(att_low, vl, NN).astype(BF16)
                g = gacc[at, hs].astype(BF16)
                mix = dot(g, vl, NT)
                sg = att * (mix - jnp.sum(mix * att, axis=-1, keepdims=True))
                sg = (sg * scale).astype(BF16)
                dv = dot(att_low, g, TN)
                dq = norm_back(dot(sg, kl, NN), qn, qs)
                dk = norm_back(dot(sg, ql, TN), kn, ks)
                for s, d, value in zip(parts, (dq, dk, dv), (q, key, v)):
                    d = d.astype(BF16)
                    dproj[at, s] = d
                    d = d.astype(F32)
                    sum_in = sum_in + d * wsum[:, s]
                    sum_cross = sum_cross + d * value
            s_in = jnp.sum(sum_in, axis=-1, keepdims=True)
            s_cross = jnp.sum(sum_cross, axis=-1, keepdims=True)
            for t in range(PATCH // HD):
                r = b * (PATCH // HD) + t
                part = slice(t * HD, (t + 1) * HD)
                rows[r : r + 1, :HD] = jnp.sum(jnp.where(eye(), s_in[part], 0.0), axis=0, keepdims=True)
                rows[r + 4 : r + 5, :HD] = jnp.sum(jnp.where(eye(), s_cross[part], 0.0), axis=0, keepdims=True)
        stats[...] = rows[...].astype(BF16)


def attend(low, grad, w):
    return pl.pallas_call(
        attend_kernel,
        grid=(8,),
        in_specs=[
            pl.BlockSpec((TOK, FEAT), lambda k: (0, k)),
            pl.BlockSpec((TOK, FEAT), lambda k: (0, k)),
            pl.BlockSpec((FEAT, WALL), lambda k: (k, 0)),
        ],
        out_specs=[whole((TOK, WA)), whole((TOK, WQ)), whole((EXTRA, FEAT))],
        out_shape=[
            jax.ShapeDtypeStruct((TOK, WA), BF16),
            jax.ShapeDtypeStruct((TOK, WQ), BF16),
            jax.ShapeDtypeStruct((EXTRA, FEAT), BF16),
        ],
        scratch_shapes=[
            pltpu.VMEM((TOK, WQ), F32),
            pltpu.VMEM((TOK, WA), F32),
            pltpu.VMEM((1, WQ), F32),
            pltpu.VMEM((EXTRA, FEAT), F32),
        ],
        compiler_params=pltpu.CompilerParams(vmem_limit_bytes=VMEM),
        cost_estimate=cost(2 * TOK * D * WALL + 8 * 2 * TOK * PATCH * WA, 16 * 1024 * 1024),
        name="attend",
    )(low, grad, w)


def store_steps(j, block, half, s_up, s_down, mids, lasts):
    for far in range(2):

        @pl.when(j == far)
        def _(far=far):
            s_up[far] = block[:half]
            s_down[far] = block[half:]

    for i, ref in enumerate(mids):

        @pl.when(j == 2 + i)
        def _(ref=ref):
            ref[...] = block

    for i, ref in enumerate(lasts):

        @pl.when(j == 6 + i)
        def _(ref=ref):
            ref[...] = block


def step_shapes(rows, width):
    half = [(2, rows // 2, width)] * 2
    return half + [(rows, width)] * 6


def token_kernel(with_stats, place, left, w, *refs):
    j = pl.program_id(0)
    outs = refs[1:] if with_stats else refs
    block = dot(left[...], w[...], NT).astype(BF16)
    if with_stats:
        block = jnp.concatenate([block, refs[0][...]], axis=0)
    store_steps(j, block, block.shape[0] // 2, outs[0], outs[1], outs[2:6], outs[6:8])


def token_blocks(place, left, w, column, stats=None):
    width = left.shape[1]
    rows = TOK + (EXTRA if stats is not None else 0)
    shapes = step_shapes(rows, FEAT)
    ins = [left, w] + ([stats] if stats is not None else [])
    return pl.pallas_call(
        functools.partial(token_kernel, stats is not None),
        grid_spec=pltpu.PrefetchScalarGridSpec(
            num_scalar_prefetch=1,
            grid=(8,),
            in_specs=[
                whole((TOK, width)),
                pl.BlockSpec((FEAT, width), lambda j, s: (s[j], column)),
            ]
            + ([whole((EXTRA, FEAT))] if stats is not None else []),
            out_specs=[whole(s) for s in shapes],
        ),
        out_shape=[jax.ShapeDtypeStruct(s, BF16) for s in shapes],
        compiler_params=params(),
        cost_estimate=cost(2 * TOK * D * width, (D * width + TOK * width + rows * D) * 2),
        name="token_blocks",
    )(place, *ins)


def weight_send_kernel(place, low_t, grad_t, dproj, attended, out):
    out[0, :, :WQ] = dot(low_t[...], dproj[...], NN).astype(BF16)
    out[0, :, WQ:] = dot(grad_t[...], attended[...], NN).astype(BF16)


def weight_keep_kernel(place, low_t, grad_t, dproj, attended, came, *outs):
    j = pl.program_id(0)
    other = came[0].astype(F32)
    block = jnp.concatenate(
        [
            (dot(low_t[...], dproj[...], NN) + other[:, :WQ]).astype(BF16),
            (dot(grad_t[...], attended[...], NN) + other[:, WQ:]).astype(BF16),
        ],
        axis=1,
    )
    store_steps(j, block, ROWS // 2, outs[0], outs[1], outs[2:6], outs[6:8])


def weight_blocks(place, low_t, grad_t, dproj, attended, came=None):
    strip = pl.BlockSpec((ROWS, TOK), lambda j, s: (s[j], 0))
    block = pl.BlockSpec((1, ROWS, WALL), lambda j, s: (j, 0, 0))
    in_specs = [strip, strip, whole((TOK, WQ)), whole((TOK, WA))]
    if came is None:
        shapes = [(8, ROWS, WALL)]
        kernel, out_specs, ins = weight_send_kernel, [block], ()
    else:
        shapes = step_shapes(ROWS, WALL)
        in_specs = in_specs + [block]
        kernel, out_specs, ins = weight_keep_kernel, [whole(s) for s in shapes], (came,)
    return pl.pallas_call(
        kernel,
        grid_spec=pltpu.PrefetchScalarGridSpec(
            num_scalar_prefetch=1, grid=(8,), in_specs=in_specs, out_specs=out_specs
        ),
        out_shape=[jax.ShapeDtypeStruct(s, BF16) for s in shapes],
        compiler_params=params(),
        cost_estimate=cost(TOK * D * WALL, 3 * D * WALL),
        name="weight_blocks",
    )(place, low_t, grad_t, dproj, attended, *ins)


def plus(*values):
    return functools.reduce(lambda a, b: a + b, [v.astype(F32) for v in values]).astype(BF16)


def reduce_ring(blocks, up, down, across):
    s_up, s_down, a1, a3, b1, b3, a0, b0 = blocks
    half = s_up.shape[1]
    from_up, from_down = up(s_up), down(s_down)
    a1 = a1.at[:half].set(plus(a1[:half], from_up[0]))
    a3 = a3.at[half:].set(plus(a3[half:], from_down[0]))
    ra, rb = up(a1), down(a3)
    b1 = b1.at[:half].set(plus(b1[:half], from_up[1]))
    b3 = b3.at[half:].set(plus(b3[half:], from_down[1]))
    rc, rd = up(b1), down(b3)
    rx = across(plus(a0, ra, rb))
    return b0, rc, rd, rx


def grads_kernel(a, b, c, d, out_in, out_out):
    total = a[...].astype(F32) + b[...].astype(F32) + c[...].astype(F32) + d[...].astype(F32)
    out_in[...] = total[:, :WQ]
    out_out[...] = total[:, WQ:]


def last_grads(parts):
    return pl.pallas_call(
        grads_kernel,
        out_shape=[jax.ShapeDtypeStruct((ROWS, WQ), F32), jax.ShapeDtypeStruct((ROWS, WA), F32)],
        compiler_params=params(),
        cost_estimate=cost(4 * ROWS * WALL, 12 * ROWS * WALL),
        name="last_grads",
    )(*parts)


def input_kernel(a, b, c, d, tokens, mean, inv, out):
    total = a[TOK:].astype(F32) + b[TOK:].astype(F32) + c[TOK:].astype(F32) + d[TOK:].astype(F32)
    for g in range(TOK // HD):
        at = slice(g * HD, (g + 1) * HD)
        value = a[at].astype(F32) + b[at].astype(F32) + c[at].astype(F32) + d[at].astype(F32)
        m_in = jnp.sum(jnp.where(eye(), total[g : g + 1, :HD], 0.0), axis=1, keepdims=True) * (1.0 / D)
        m_cross = jnp.sum(jnp.where(eye(), total[g + 4 : g + 5, :HD], 0.0), axis=1, keepdims=True) * (1.0 / D)
        i = inv[at]
        normed = (tokens[at].astype(F32) - mean[at]) * i
        out[at] = (i * (value - m_in - normed * m_cross)).astype(BF16)


def last_input(parts, tokens, mean, inv):
    return pl.pallas_call(
        input_kernel,
        out_shape=jax.ShapeDtypeStruct((TOK, FEAT), BF16),
        compiler_params=params(),
        cost_estimate=cost(12 * TOK * FEAT, 12 * TOK * FEAT),
        name="last_input",
    )(*parts, tokens, mean, inv)


def local(tokens, update_grad, weight_in, weight_out):
    m = lax.axis_index("mp")
    x, y = m // 4, m % 4
    d = lax.axis_index("dp")
    z, near, core = d // 4, (d // 2) % 2, d % 2
    place_in = jnp.stack([((x + a) % 2) * 4 + (y + b) % 4 for a, b in PIECES]).astype(jnp.int32)
    place_tok = jnp.stack([((x + a) % 2) * 4 + (y + b) % 4 for a, b in BLOCKS]).astype(jnp.int32)
    strips = [((z + b) % 4) * 4 + ((near + a) % 2) * 2 for a, b in BLOCKS]
    place_keep = jnp.stack([s + core for s in strips]).astype(jnp.int32)
    place_send = jnp.stack([s + 1 - core for s in strips]).astype(jnp.int32)

    w = lax.all_gather(jnp.concatenate([weight_in, weight_out], axis=1), "dp", axis=0, tiled=True)

    own = jnp.stack([tokens, update_grad])
    ap, am = y_up(own), y_down(own)
    xx = x_far(own)
    bp, bm = y_up(xx), y_down(xx)
    fat, fag = y_up(ap[0]), y_down(am[1])
    fbt, fbg = y_up(bp[0]), y_down(bm[1])

    low, grad, low_t, grad_t, mean, inv = prep(place_in, (own, ap, am, fat, fag, xx, bp, bm, fbt, fbg))
    attended, dproj, stats = attend(low, grad, w)

    update_parts = reduce_ring(token_blocks(place_tok, attended, w, 3), y_up, y_down, x_far)
    update = plus(*update_parts)

    (send,) = weight_blocks(place_send, low_t, grad_t, dproj, attended)
    came = other_core(send)
    normed_blocks = token_blocks(place_tok, dproj, w, 0, stats)
    keep = weight_blocks(place_keep, low_t, grad_t, dproj, attended, came)
    grad_parts = reduce_ring(keep, z_up, z_down, x_near)
    input_parts = reduce_ring(normed_blocks, y_up, y_down, x_far)
    weight_in_grad, weight_out_grad = last_grads(grad_parts)
    input_grad = last_input(input_parts, tokens, mean, inv)
    return (update, input_grad, weight_in_grad, weight_out_grad)


def solution(mesh):
    return jax.shard_map(
        local,
        mesh=mesh,
        in_specs=(P("dp", "mp"), P("dp", "mp"), P("dp", "mp"), P("dp", "mp")),
        out_specs=(P("dp", "mp"), P("dp", "mp"), P("dp", "mp"), P("dp", "mp")),
        check_vma=False,
    )
```

time: 581 us -> 244 us (0.42)
  waiting for transfers between devices: 448 us -> 91.5 us
  Pallas kernels: 0 us -> 76.3 us
  matrix products: 53.8 us -> 0 us
  starting transfers between devices: 0.49 us -> 48 us
  local copies, waits for them, and re-layouts: 36.7 us -> 7.97 us
  other arithmetic: 27.1 us -> 4.79 us
    all_gather x4 -> x1, waiting for transfers between devices: 204 us -> 0.02 us  [local(): lax.all_gather(jnp.concatenate([weight_in, weight_out], axis=1), 'dp', ax...]
    unnamed x9 -> x1, waiting for transfers between devices: 186 us -> 0.02 us
    ppermute x0 -> x31, waiting for transfers between devices: none -> 91.4 us  [the longest x3 36.6 us: x_far(): return lax.ppermute(v, 'mp', mp_perm(1, 0))]
    pallas_call x0 -> x8, Pallas kernels: none -> 76.3 us  [the longest x2 21.4 us: weight_blocks(): pl.pallas_call(kernel, grid_spec=pltpu.PrefetchScalarGridSpec(num_scalar_...]
    psum x1 -> x0, waiting for transfers between devices: 58.1 us -> none  [local(): lax.psum(normed_grad.astype(jnp.bfloat16), 'mp').astype(jnp.float32)]
    dot_general x11 -> x0, matrix products: 50.6 us -> none  [the longest x1 8.78 us: local(): jnp.einsum('tc,dc->td', projected_grad, whole_in, preferred_element_type=...]
    ppermute x0 -> x31, starting transfers between devices: none -> 48 us  [the longest x10 19.1 us: y_down(): return lax.ppermute(v, 'mp', mp_perm(0, 3))]
    unnamed x37 -> x66, local copies, waits for them, and re-layouts: 24.8 us -> 2.8 us
  transfers between devices with their start and end apart: 7 -> 32, of which waited for: 7 -> 12; matrix products, arithmetic and copies ran while one was open for 10% -> 3% of each run, Pallas kernels for 0% -> 19%
where the time goes in v1:
time: 244 us; the launch traced here: 243 us
  waiting for transfers between devices  91.5 us (38%)
  Pallas kernels  76.3 us (31%)
  starting transfers between devices  48 us (20%)
  between operations  14.4 us (6%)
  local copies, waits for them, and re-layouts  7.97 us (3%)
  other arithmetic  4.79 us (2%)
    ppermute x3, waiting for transfers between devices, x_far(): return lax.ppermute(v, 'mp', mp_perm(1, 0))  36.6 us
    ppermute x10, waiting for transfers between devices, y_up(): return lax.ppermute(v, 'mp', mp_perm(0, 1))  29.3 us
    pallas_call x2, Pallas kernels, weight_blocks(): pl.pallas_call(kernel, grid_spec=pltpu.PrefetchScalarGridSpec(num_scalar_...  21.4 us
    pallas_call x2, Pallas kernels, token_blocks(): pl.pallas_call(functools.partial(token_kernel, stats is not None), grid_s...  21.3 us
    ppermute x10, starting transfers between devices, y_down(): return lax.ppermute(v, 'mp', mp_perm(0, 3))  19.1 us
    pallas_call x1, Pallas kernels, attend(): pl.pallas_call(attend_kernel, grid=(8,), in_specs=[pl.BlockSpec((TOK, FEA...  17.7 us
    ppermute x3, waiting for transfers between devices, z_up(): return lax.ppermute(v, 'dp', dp_perm(1, 0, 0))  15.4 us
    ppermute x3, starting transfers between devices, x_far(): return lax.ppermute(v, 'mp', mp_perm(1, 0))  10.6 us
  transfers between devices with their start and end apart: 32, of which 12 were waited for; matrix products, arithmetic and copies ran while one was open for 3% of the time, Pallas kernels for 19%

profile of v1, /device:TPU:0, one launch (start us, length us, event | category | flops | bytes accessed | tf_op | source)
XLA Modules:
  0.0 242.9 jit_solution(8189216311357823851)
XLA Ops:
  7.2 2.0 pad_maximum_fusion.1
  9.4 3.2 %collective-permute-start.4 = (bf16[2,512,384]{2,1,0:T(8,128)(2,1)S(1)}, bf16[2,512,384]{2,1,0:T(8,128)(2,1)S(1)}, u32[]{:S(2)}, u32[]{:S(2)}) collective-permute-start(bf16[2,512,384]{2,1,0:T(8,128)(2,1)S(1)} %pad_maximum_fusion.own), channel_id=1, source_target_pairs={{0,4},{1,5},{2,6},{3,7},{4,0},{5,1},{6,2},{7,3},{8,12},{9,13},{10,... | collective-permute-start | bytes 2359304 | tf_op jit(solution)/shard_map/ppermute | solution.py:61
  14.2 1.7 collective-permute-start.1
  15.8 22.9 %collective-permute-done.4.xx = bf16[2,512,384]{2,1,0:T(8,128)(2,1)S(1)} collective-permute-done((bf16[2,512,384]{2,1,0:T(8,128)(2,1)S(1)}, bf16[2,512,384]{2,1,0:T(8,128)(2,1)S(1)}, u32[]{:S(2)}, u32[]{:S(2)}) %collective-permute-start.4) | collective-permute-done | bytes 786464 | tf_op jit(solution)/shard_map/ppermute | solution.py:61
  40.2 1.8 collective-permute-start.6
  43.9 3.0 %collective-permute-start.3 = (bf16[512,384]{1,0:T(8,128)(2,1)}, bf16[512,384]{1,0:T(8,128)(2,1)}, u32[]{:S(2)}, u32[]{:S(2)}) collective-permute-start(bf16[512,384]{1,0:T(8,128)(2,1)} %slice_bitcast_fusion.2), channel_id=1, source_target_pairs={{0,3},{1,0},{2,1},{3,2},{4,7},{5,4},{6,5},{7,6},{8,11},{9,8},{10,9... | collective-permute-start | bytes 1179656 | tf_op jit(solution)/shard_map/ppermute | solution.py:57
  46.9 13.5 %collective-permute-done.5.bp = bf16[2,512,384]{2,1,0:T(8,128)(2,1)S(1)} collective-permute-done((bf16[2,512,384]{2,1,0:T(8,128)(2,1)S(1)}, bf16[2,512,384]{2,1,0:T(8,128)(2,1)S(1)}, u32[]{:S(2)}, u32[]{:S(2)}) %collective-permute-start.5) | collective-permute-done | bytes 786464 | tf_op jit(solution)/shard_map/ppermute | solution.py:53
  61.6 3.1 %collective-permute-start.8 = (bf16[512,384]{1,0:T(8,128)(2,1)S(1)}, bf16[512,384]{1,0:T(8,128)(2,1)S(1)}, u32[]{:S(2)}, u32[]{:S(2)}) collective-permute-start(bf16[512,384]{1,0:T(8,128)(2,1)S(1)} %slice_bitcast_fusion), channel_id=1, source_target_pairs={{0,3},{1,0},{2,1},{3,2},{4,7},{5,4},{6,5},{7,6},{8,11},{9,8},{10,9... | collective-permute-start | bytes 1179656 | tf_op jit(solution)/shard_map/ppermute | solution.py:57
  65.9 2.9 %collective-permute-done.2.fat = bf16[512,384]{1,0:T(8,128)(2,1)S(1)} collective-permute-done((bf16[512,384]{1,0:T(8,128)(2,1)}, bf16[512,384]{1,0:T(8,128)(2,1)S(1)}, u32[]{:S(2)}, u32[]{:S(2)}) %collective-permute-start.2) | collective-permute-done | bytes 393248 | tf_op jit(solution)/shard_map/ppermute | solution.py:53
  68.8 4.3 %collective-permute-done.7.fbt = bf16[512,384]{1,0:T(8,128)(2,1)} collective-permute-done((bf16[512,384]{1,0:T(8,128)(2,1)}, bf16[512,384]{1,0:T(8,128)(2,1)}, u32[]{:S(2)}, u32[]{:S(2)}) %collective-permute-start.7) | collective-permute-done | bytes 393248 | tf_op jit(solution)/shard_map/ppermute | solution.py:53
  73.9 10.2 %prep.1 = (bf16[512,3072]{1,0:T(8,128)(2,1)}, bf16[512,3072]{1,0:T(8,128)(2,1)}, bf16[3072,512]{1,0:T(8,128)(2,1)}, bf16[3072,512]{1,0:T(8,128)(2,1)}, f32[512,1]{1,0:T(8,128)}, /*index=5*/f32[512,1]{1,0:T(8,128)}) custom-call(s32[8]{0:T(128)} %stack.110.place, bf16[2,512,384]{2,1,0:T(8,128)(2,1)} %copy-done, bf16[2,512,384]{2,1,0:T(8,128)(2,1)} %copy-done.1, ...), custom_call_target="tpu_custom_call" | custom-call | flops 31457280 | bytes 18874368 | tf_op jit(solution)/shard_map/prep/pallas_call | solution.py:137
  84.1 17.7 %attend.1 = (bf16[512,384]{1,0:T(8,128)(2,1)}, bf16[512,1152]{1,0:T(8,128)(2,1)}, bf16[32,384]{1,0:T(8,128)(2,1)}) custom-call(bf16[512,3072]{1,0:T(8,128)(2,1)} %get-tuple-element.183.low, bf16[512,3072]{1,0:T(8,128)(2,1)} %get-tuple-element.184.grad, bf16[3072,1536]{1,0:T(8,128)(2,1)} %all-gather.2.cloned.1.call-done.w), custom_call_target="tpu_custom_call" | custom-call | flops 5637144576 | bytes 16777216 | tf_op jit(solution)/shard_map/attend/pallas_call | solution.py:220
  101.9 9.7 %weight_blocks.2 = bf16[8,192,1536]{2,1,0:T(8,128)(2,1)} custom-call(s32[8]{0:T(128)} %stack.131.place, bf16[3072,512]{1,0:T(8,128)(2,1)} %get-tuple-element.206.low_t, bf16[3072,512]{1,0:T(8,128)(2,1)} %get-tuple-element.207.grad_t, bf16[512,1152]{1,0:T(8,128)(2,1)} %get-tuple-element.194.left.dproj, bf16[512,384]{1,0:T(8,128)(2,1)} %get-tuple-element.185.left.attended), custom_call_target="tpu_custom_call" | custom-call | flops 2415919104 | bytes 14155776 | tf_op jit(solution)/shard_map/weight_blocks/pallas_call | solution.py:334
  112.9 8.9 %token_blocks.2 = (bf16[2,256,384]{2,1,0:T(8,128)(2,1)}, bf16[2,256,384]{2,1,0:T(8,128)(2,1)}, bf16[512,384]{1,0:T(8,128)(2,1)}, bf16[512,384]{1,0:T(8,128)(2,1)...) custom-call(s32[8]{0:T(128)} %stack.109.place, ...), custom_call_target="tpu_custom_call" | custom-call | flops 1207959552 | bytes 5898240 | tf_op jit(solution)/shard_map/token_blocks/pallas_call | solution.py:286
  121.7 2.8 %collective-permute-start.11 = (bf16[2,256,384]{2,1,0:T(8,128)(2,1)}, bf16[2,256,384]{2,1,0:T(8,128)(2,1)S(1)}, u32[]{:S(2)}, u32[]{:S(2)}) collective-permute-start(bf16[2,256,384]{2,1,0:T(8,128)(2,1)} %get-tuple-element.190), channel_id=1, source_target_pairs={{0,3},{1,0},{2,1},{3,2},{4,7},{5,4},{6,5},{7,6},{8,11},{9,8},{10,9... | collective-permute-start | bytes 1179656 | tf_op jit(solution)/shard_map/ppermute | solution.py:57
  124.6 11.7 %weight_blocks.3 = (bf16[2,96,1536]{2,1,0:T(8,128)(2,1)}, bf16[2,96,1536]{2,1,0:T(8,128)(2,1)}, bf16[192,1536]{1,0:T(8,128)(2,1)}, bf16[192,1536]{1,0:T(8,128)(2...) custom-call(s32[8]{0:T(128)} %stack.122.place, ...), custom_call_target="tpu_custom_call" | custom-call | flops 2415919104 | bytes 14155776 | tf_op jit(solution)/shard_map/weight_blocks/pallas_call | solution.py:334
  136.3 5.1 %collective-permute-start.26 = (bf16[2,96,1536]{2,1,0:T(8,128)(2,1)}, bf16[2,96,1536]{2,1,0:T(8,128)(2,1)S(1)}, u32[]{:S(2)}, u32[]{:S(2)}) collective-permute-start(bf16[2,96,1536]{2,1,0:T(8,128)(2,1)} %get-tuple-element.212), channel_id=1, source_target_pairs={{0,96},{8,104},{16,112},{24,120},{32,0},{40,8},{48,16},{56,24},{64... | collective-permute-start | bytes 1769480 | tf_op jit(solution)/shard_map/ppermute | solution.py:69
  141.4 12.4 %token_blocks.3 = (bf16[2,272,384]{2,1,0:T(8,128)(2,1)}, bf16[2,272,384]{2,1,0:T(8,128)(2,1)}, bf16[544,384]{1,0:T(8,128)(2,1)}, bf16[544,384]{1,0:T(8,128)(2,1)...) custom-call(s32[8]{0:T(128)} %stack.109.place, ...), custom_call_target="tpu_custom_call" | custom-call | flops 3623878656 | bytes 11599872 | tf_op jit(solution)/shard_map/token_blocks/pallas_call | solution.py:286
  154.4 2.8 %collective-permute-start.18 = (bf16[2,272,384]{2,1,0:T(8,128)(2,1)}, bf16[2,272,384]{2,1,0:T(8,128)(2,1)S(1)}, u32[]{:S(2)}, u32[]{:S(2)}) collective-permute-start(bf16[2,272,384]{2,1,0:T(8,128)(2,1)} %get-tuple-element.200), channel_id=1, source_target_pairs={{0,3},{1,0},{2,1},{3,2},{4,7},{5,4},{6,5},{7,6},{8,11},{9,8},{10,9... | collective-permute-start | bytes 1253384 | tf_op jit(solution)/shard_map/ppermute | solution.py:57
  157.4 2.0 collective-permute-start.14
  160.1 14.6 %collective-permute-done.24 = bf16[2,96,1536]{2,1,0:T(8,128)(2,1)S(1)} collective-permute-done((bf16[2,96,1536]{2,1,0:T(8,128)(2,1)S(1)}, bf16[2,96,1536]{2,1,0:T(8,128)(2,1)S(1)}, u32[]{:S(2)}, u32[]{:S(2)}) %collective-permute-start.24) | collective-permute-done | bytes 589856 | tf_op jit(solution)/shard_map/ppermute | solution.py:65
  174.9 2.1 collective-permute-start.28
  177.9 1.7 collective-permute-start.10
  180.2 6.4 %collective-permute-done.12 = bf16[512,384]{1,0:T(8,128)(2,1)S(1)} collective-permute-done((bf16[512,384]{1,0:T(8,128)(2,1)S(1)}, bf16[512,384]{1,0:T(8,128)(2,1)S(1)}, u32[]{:S(2)}, u32[]{:S(2)}) %collective-permute-start.12) | collective-permute-done | bytes 393248 | tf_op jit(solution)/shard_map/ppermute | solution.py:57
  189.4 4.0 %collective-permute-start.15 = (bf16[512,384]{1,0:T(8,128)(2,1)S(1)}, bf16[512,384]{1,0:T(8,128)(2,1)S(1)}, u32[]{:S(2)}, u32[]{:S(2)}) collective-permute-start(bf16[512,384]{1,0:T(8,128)(2,1)S(1)} %add_convert_fusion.3), channel_id=1, source_target_pairs={{0,4},{1,5},{2,6},{3,7},{4,0},{5,1},{6,2},{7,3},{8,12},{9,13},{10,... | collective-permute-start | bytes 1179656 | tf_op jit(solution)/shard_map/ppermute | solution.py:61
  194.7 2.2 collective-permute-start.27
  196.9 8.6 %collective-permute-done.20 = bf16[544,384]{1,0:T(8,128)(2,1)S(1)} collective-permute-done((bf16[544,384]{1,0:T(8,128)(2,1)S(1)}, bf16[544,384]{1,0:T(8,128)(2,1)S(1)}, u32[]{:S(2)}, u32[]{:S(2)}) %collective-permute-start.20) | collective-permute-done | bytes 417824 | tf_op jit(solution)/shard_map/ppermute | solution.py:53
  207.1 3.4 %collective-permute-start.22 = (bf16[544,384]{1,0:T(8,128)(2,1)S(1)}, bf16[544,384]{1,0:T(8,128)(2,1)S(1)}, u32[]{:S(2)}, u32[]{:S(2)}) collective-permute-start(bf16[544,384]{1,0:T(8,128)(2,1)S(1)} %add_convert_fusion.1), channel_id=1, source_target_pairs={{0,4},{1,5},{2,6},{3,7},{4,0},{5,1},{6,2},{7,3},{8,12},{9,13},{10,... | collective-permute-start | bytes 1253384 | tf_op jit(solution)/shard_map/ppermute | solution.py:61
  211.5 3.2 %collective-permute-done.19.c = bf16[544,384]{1,0:T(8,128)(2,1)S(1)} collective-permute-done((bf16[544,384]{1,0:T(8,128)(2,1)S(1)}, bf16[544,384]{1,0:T(8,128)(2,1)S(1)}, u32[]{:S(2)}, u32[]{:S(2)}) %collective-permute-start.19) | collective-permute-done | bytes 417824 | tf_op jit(solution)/shard_map/ppermute | solution.py:57
  214.7 13.7 %collective-permute-done.22.d = bf16[544,384]{1,0:T(8,128)(2,1)S(1)} collective-permute-done((bf16[544,384]{1,0:T(8,128)(2,1)S(1)}, bf16[544,384]{1,0:T(8,128)(2,1)S(1)}, u32[]{:S(2)}, u32[]{:S(2)}) %collective-permute-start.22) | collective-permute-done | bytes 417824 | tf_op jit(solution)/shard_map/ppermute | solution.py:61
  229.1 2.9 %last_input.1 = bf16[512,384]{1,0:T(8,128)(2,1)} custom-call(bf16[544,384]{1,0:T(8,128)(2,1)} %get-tuple-element.196.a, bf16[544,384]{1,0:T(8,128)(2,1)} %copy-done.12, bf16[544,384]{1,0:T(8,128)(2,1)} %copy-done.13, bf16[544,384]{1,0:T(8,128)(2,1)} %copy-done.14, bf16[512,384]{1,0:T(8,128)(2,1)} %tokens.1, f32[512,1]{1,0:T(8,128)} %get-tuple-element.204.mean, ...), custom_call_target="tpu_custom_call" | custom-call | flops 2359296 | bytes 2359296 | tf_op jit(solution)/shard_map/last_input/pallas_call | solution.py:393
  233.2 2.8 %last_grads.1 = (f32[192,1152]{1,0:T(8,128)}, f32[192,384]{1,0:T(8,128)}) custom-call(bf16[192,1536]{1,0:T(8,128)(2,1)} %get-tuple-element.208.a, bf16[192,1536]{1,0:T(8,128)(2,1)} %copy-done.8, bf16[192,1536]{1,0:T(8,128)(2,1)} %copy-done.9, bf16[192,1536]{1,0:T(8,128)(2,1)} %copy-done.10), custom_call_target="tpu_custom_call" | custom-call | flops 1179648 | bytes 3538944 | tf_op jit(solution)/shard_map/last_grads/pallas_call | solution.py:371
  (127 shorter events, 21.1 us)
Async XLA Ops:
  7.2 76.9 %all-gather.2.cloned.1.call-start = ((), (), s32[]{:S(2)}) async-start(), calls=%async_computation | async-start | bytes 10027008 | tf_op jit(solution)/shard_map/all_gather | solution.py:413
  9.4 29.3 %collective-permute-start.4 = (bf16[2,512,384]{2,1,0:T(8,128)(2,1)S(1)}, bf16[2,512,384]{2,1,0:T(8,128)(2,1)S(1)}, u32[]{:S(2)}, u32[]{:S(2)}) collective-permute-start(bf16[2,512,384]{2,1,0:T(8,128)(2,1)S(1)} %pad_maximum_fusion.own), channel_id=1, source_target_pairs={{0,4},{1,5},{2,6},{3,7},{4,0},{5,1},{6,2},{7,3},{8,12},{9,13},{10,... | collective-permute-start | bytes 2359304 | tf_op jit(solution)/shard_map/ppermute | solution.py:61
  12.6 29.4 %collective-permute-start = (bf16[2,512,384]{2,1,0:T(8,128)(2,1)S(1)}, bf16[2,512,384]{2,1,0:T(8,128)(2,1)S(1)}, u32[]{:S(2)}, u32[]{:S(2)}) collective-permute-start(bf16[2,512,384]{2,1,0:T(8,128)(2,1)S(1)} %pad_maximum_fusion.own), channel_id=1, source_target_pairs={{0,1},{1,2},{2,3},{3,0},{4,5},{5,6},{6,7},{7,4},{8,9},{9,10},{10,1... | collective-permute-start | bytes 2359304 | tf_op jit(solution)/shard_map/ppermute | solution.py:53
  14.2 28.9 %collective-permute-start.1 = (bf16[2,512,384]{2,1,0:T(8,128)(2,1)S(1)}, bf16[2,512,384]{2,1,0:T(8,128)(2,1)S(1)}, u32[]{:S(2)}, u32[]{:S(2)}) collective-permute-start(bf16[2,512,384]{2,1,0:T(8,128)(2,1)S(1)} %pad_maximum_fusion.own), channel_id=1, source_target_pairs={{0,3},{1,0},{2,1},{3,2},{4,7},{5,4},{6,5},{7,6},{8,11},{9,8},{10,9... | collective-permute-start | bytes 2359304 | tf_op jit(solution)/shard_map/ppermute | solution.py:57
  38.8 21.7 %collective-permute-start.5 = (bf16[2,512,384]{2,1,0:T(8,128)(2,1)S(1)}, bf16[2,512,384]{2,1,0:T(8,128)(2,1)S(1)}, u32[]{:S(2)}, u32[]{:S(2)}) collective-permute-start(bf16[2,512,384]{2,1,0:T(8,128)(2,1)S(1)} %collective-permute-done.4.xx), channel_id=1, source_target_pairs={{0,1},{1,2},{2,3},{3,0},{4,5},{5,6},{6,7},{7,4},{8,9},{9,10},{10,1... | collective-permute-start | bytes 2359304 | tf_op jit(solution)/shard_map/ppermute | solution.py:53
  40.2 21.4 %collective-permute-start.6 = (bf16[2,512,384]{2,1,0:T(8,128)(2,1)S(1)}, bf16[2,512,384]{2,1,0:T(8,128)(2,1)S(1)}, u32[]{:S(2)}, u32[]{:S(2)}) collective-permute-start(bf16[2,512,384]{2,1,0:T(8,128)(2,1)S(1)} %collective-permute-done.4.xx), channel_id=1, source_target_pairs={{0,3},{1,0},{2,1},{3,2},{4,7},{5,4},{6,5},{7,6},{8,11},{9,8},{10,9... | collective-permute-start | bytes 2359304 | tf_op jit(solution)/shard_map/ppermute | solution.py:57
  42.8 26.0 %collective-permute-start.2 = (bf16[512,384]{1,0:T(8,128)(2,1)}, bf16[512,384]{1,0:T(8,128)(2,1)S(1)}, u32[]{:S(2)}, u32[]{:S(2)}) collective-permute-start(bf16[512,384]{1,0:T(8,128)(2,1)} %slice_bitcast_fusion.3), channel_id=1, source_target_pairs={{0,1},{1,2},{2,3},{3,0},{4,5},{5,6},{6,7},{7,4},{8,9},{9,10},{10,1... | collective-permute-start | bytes 1179656 | tf_op jit(solution)/shard_map/ppermute | solution.py:53
  43.9 24.9 %collective-permute-start.3 = (bf16[512,384]{1,0:T(8,128)(2,1)}, bf16[512,384]{1,0:T(8,128)(2,1)}, u32[]{:S(2)}, u32[]{:S(2)}) collective-permute-start(bf16[512,384]{1,0:T(8,128)(2,1)} %slice_bitcast_fusion.2), channel_id=1, source_target_pairs={{0,3},{1,0},{2,1},{3,2},{4,7},{5,4},{6,5},{7,6},{8,11},{9,8},{10,9... | collective-permute-start | bytes 1179656 | tf_op jit(solution)/shard_map/ppermute | solution.py:57
  61.3 11.8 %collective-permute-start.7 = (bf16[512,384]{1,0:T(8,128)(2,1)}, bf16[512,384]{1,0:T(8,128)(2,1)}, u32[]{:S(2)}, u32[]{:S(2)}) collective-permute-start(bf16[512,384]{1,0:T(8,128)(2,1)} %slice_bitcast_fusion.1), channel_id=1, source_target_pairs={{0,1},{1,2},{2,3},{3,0},{4,5},{5,6},{6,7},{7,4},{8,9},{9,10},{10,1... | collective-permute-start | bytes 1179656 | tf_op jit(solution)/shard_map/ppermute | solution.py:53
  61.6 11.5 %collective-permute-start.8 = (bf16[512,384]{1,0:T(8,128)(2,1)S(1)}, bf16[512,384]{1,0:T(8,128)(2,1)S(1)}, u32[]{:S(2)}, u32[]{:S(2)}) collective-permute-start(bf16[512,384]{1,0:T(8,128)(2,1)S(1)} %slice_bitcast_fusion), channel_id=1, source_target_pairs={{0,3},{1,0},{2,1},{3,2},{4,7},{5,4},{6,5},{7,6},{8,11},{9,8},{10,9... | collective-permute-start | bytes 1179656 | tf_op jit(solution)/shard_map/ppermute | solution.py:57
  111.6 13.0 %collective-permute-start.23 = (bf16[8,192,1536]{2,1,0:T(8,128)(2,1)}, bf16[8,192,1536]{2,1,0:T(8,128)(2,1)}, u32[]{:S(2)}, u32[]{:S(2)}) collective-permute-start(bf16[8,192,1536]{2,1,0:T(8,128)(2,1)} %weight_blocks.2), channel_id=1, source_target_pairs={{0,8},{8,0},{16,24},{24,16},{32,40},{40,32},{48,56},{56,48},{64,72... | collective-permute-start | bytes 14155784 | tf_op jit(solution)/shard_map/ppermute | solution.py:77
  121.7 35.5 %collective-permute-start.11 = (bf16[2,256,384]{2,1,0:T(8,128)(2,1)}, bf16[2,256,384]{2,1,0:T(8,128)(2,1)S(1)}, u32[]{:S(2)}, u32[]{:S(2)}) collective-permute-start(bf16[2,256,384]{2,1,0:T(8,128)(2,1)} %get-tuple-element.190), channel_id=1, source_target_pairs={{0,3},{1,0},{2,1},{3,2},{4,7},{5,4},{6,5},{7,6},{8,11},{9,8},{10,9... | collective-permute-start | bytes 1179656 | tf_op jit(solution)/shard_map/ppermute | solution.py:57
  124.6 34.9 %collective-permute-start.9 = (bf16[2,256,384]{2,1,0:T(8,128)(2,1)}, bf16[2,256,384]{2,1,0:T(8,128)(2,1)S(1)}, u32[]{:S(2)}, u32[]{:S(2)}) collective-permute-start(bf16[2,256,384]{2,1,0:T(8,128)(2,1)} %get-tuple-element.188), channel_id=1, source_target_pairs={{0,1},{1,2},{2,3},{3,0},{4,5},{5,6},{6,7},{7,4},{8,9},{9,10},{10,1... | collective-permute-start | bytes 1179656 | tf_op jit(solution)/shard_map/ppermute | solution.py:53
  136.3 23.4 %collective-permute-start.26 = (bf16[2,96,1536]{2,1,0:T(8,128)(2,1)}, bf16[2,96,1536]{2,1,0:T(8,128)(2,1)S(1)}, u32[]{:S(2)}, u32[]{:S(2)}) collective-permute-start(bf16[2,96,1536]{2,1,0:T(8,128)(2,1)} %get-tuple-element.212), channel_id=1, source_target_pairs={{0,96},{8,104},{16,112},{24,120},{32,0},{40,8},{48,16},{56,24},{64... | collective-permute-start | bytes 1769480 | tf_op jit(solution)/shard_map/ppermute | solution.py:69
  153.8 21.1 %collective-permute-start.16 = (bf16[2,272,384]{2,1,0:T(8,128)(2,1)}, bf16[2,272,384]{2,1,0:T(8,128)(2,1)S(1)}, u32[]{:S(2)}, u32[]{:S(2)}) collective-permute-start(bf16[2,272,384]{2,1,0:T(8,128)(2,1)} %get-tuple-element.198), channel_id=1, source_target_pairs={{0,1},{1,2},{2,3},{3,0},{4,5},{5,6},{6,7},{7,4},{8,9},{9,10},{10,1... | collective-permute-start | bytes 1253384 | tf_op jit(solution)/shard_map/ppermute | solution.py:53
  154.4 22.8 %collective-permute-start.18 = (bf16[2,272,384]{2,1,0:T(8,128)(2,1)}, bf16[2,272,384]{2,1,0:T(8,128)(2,1)S(1)}, u32[]{:S(2)}, u32[]{:S(2)}) collective-permute-start(bf16[2,272,384]{2,1,0:T(8,128)(2,1)} %get-tuple-element.200), channel_id=1, source_target_pairs={{0,3},{1,0},{2,1},{3,2},{4,7},{5,4},{6,5},{7,6},{8,11},{9,8},{10,9... | collective-permute-start | bytes 1253384 | tf_op jit(solution)/shard_map/ppermute | solution.py:57
  157.4 20.5 %collective-permute-start.14 = (bf16[512,384]{1,0:T(8,128)(2,1)S(1)}, bf16[512,384]{1,0:T(8,128)(2,1)S(1)}, u32[]{:S(2)}, u32[]{:S(2)}) collective-permute-start(bf16[512,384]{1,0:T(8,128)(2,1)S(1)} %get-tuple-element.229), channel_id=1, source_target_pairs={{0,3},{1,0},{2,1},{3,2},{4,7},{5,4},{6,5},{7,6},{8,11},{9,8},{10,9... | collective-permute-start | bytes 1179656 | tf_op jit(solution)/shard_map/ppermute | solution.py:57
  159.5 15.3 %collective-permute-start.24 = (bf16[2,96,1536]{2,1,0:T(8,128)(2,1)S(1)}, bf16[2,96,1536]{2,1,0:T(8,128)(2,1)S(1)}, u32[]{:S(2)}, u32[]{:S(2)}) collective-permute-start(bf16[2,96,1536]{2,1,0:T(8,128)(2,1)S(1)} %copy-done.32), channel_id=1, source_target_pairs={{0,32},{8,40},{16,48},{24,56},{32,64},{40,72},{48,80},{56,88},{64,... | collective-permute-start | bytes 1769480 | tf_op jit(solution)/shard_map/ppermute | solution.py:65
  159.7 19.9 %collective-permute-start.13 = (bf16[512,384]{1,0:T(8,128)(2,1)S(1)}, bf16[512,384]{1,0:T(8,128)(2,1)S(1)}, u32[]{:S(2)}, u32[]{:S(2)}) collective-permute-start(bf16[512,384]{1,0:T(8,128)(2,1)S(1)} %get-tuple-element.227), channel_id=1, source_target_pairs={{0,1},{1,2},{2,3},{3,0},{4,5},{5,6},{6,7},{7,4},{8,9},{9,10},{10,1... | collective-permute-start | bytes 1179656 | tf_op jit(solution)/shard_map/ppermute | solution.py:53
  174.7 13.1 %collective-permute-start.29 = (bf16[192,1536]{1,0:T(8,128)(2,1)S(1)}, bf16[192,1536]{1,0:T(8,128)(2,1)S(1)}, u32[]{:S(2)}, u32[]{:S(2)}) collective-permute-start(bf16[192,1536]{1,0:T(8,128)(2,1)S(1)} %get-tuple-element.220), channel_id=1, source_target_pairs={{0,96},{8,104},{16,112},{24,120},{32,0},{40,8},{48,16},{56,24},{64... | collective-permute-start | bytes 1769480 | tf_op jit(solution)/shard_map/ppermute | solution.py:69
  174.9 14.4 %collective-permute-start.28 = (bf16[192,1536]{1,0:T(8,128)(2,1)S(1)}, bf16[192,1536]{1,0:T(8,128)(2,1)S(1)}, u32[]{:S(2)}, u32[]{:S(2)}) collective-permute-start(bf16[192,1536]{1,0:T(8,128)(2,1)S(1)} %get-tuple-element.218), channel_id=1, source_target_pairs={{0,32},{8,40},{16,48},{24,56},{32,64},{40,72},{48,80},{56,88},{64,... | collective-permute-start | bytes 1769480 | tf_op jit(solution)/shard_map/ppermute | solution.py:65
  177.3 9.3 %collective-permute-start.12 = (bf16[512,384]{1,0:T(8,128)(2,1)S(1)}, bf16[512,384]{1,0:T(8,128)(2,1)S(1)}, u32[]{:S(2)}, u32[]{:S(2)}) collective-permute-start(bf16[512,384]{1,0:T(8,128)(2,1)S(1)} %get-tuple-element.228), channel_id=1, source_target_pairs={{0,3},{1,0},{2,1},{3,2},{4,7},{5,4},{6,5},{7,6},{8,11},{9,8},{10,9... | collective-permute-start | bytes 1179656 | tf_op jit(solution)/shard_map/ppermute | solution.py:57
  177.9 15.6 %collective-permute-start.10 = (bf16[512,384]{1,0:T(8,128)(2,1)S(1)}, bf16[512,384]{1,0:T(8,128)(2,1)S(1)}, u32[]{:S(2)}, u32[]{:S(2)}) collective-permute-start(bf16[512,384]{1,0:T(8,128)(2,1)S(1)} %get-tuple-element.226), channel_id=1, source_target_pairs={{0,1},{1,2},{2,3},{3,0},{4,5},{5,6},{6,7},{7,4},{8,9},{9,10},{10,1... | collective-permute-start | bytes 1179656 | tf_op jit(solution)/shard_map/ppermute | solution.py:53
  179.7 26.9 %collective-permute-start.17 = (bf16[544,384]{1,0:T(8,128)(2,1)S(1)}, bf16[544,384]{1,0:T(8,128)(2,1)S(1)}, u32[]{:S(2)}, u32[]{:S(2)}) collective-permute-start(bf16[544,384]{1,0:T(8,128)(2,1)S(1)} %get-tuple-element.223), channel_id=1, source_target_pairs={{0,1},{1,2},{2,3},{3,0},{4,5},{5,6},{6,7},{7,4},{8,9},{9,10},{10,1... | collective-permute-start | bytes 1253384 | tf_op jit(solution)/shard_map/ppermute | solution.py:53
  186.6 8.0 %collective-permute-start.21 = (bf16[544,384]{1,0:T(8,128)(2,1)S(1)}, bf16[544,384]{1,0:T(8,128)(2,1)S(1)}, u32[]{:S(2)}, u32[]{:S(2)}) collective-permute-start(bf16[544,384]{1,0:T(8,128)(2,1)S(1)} %get-tuple-element.224), channel_id=1, source_target_pairs={{0,3},{1,0},{2,1},{3,2},{4,7},{5,4},{6,5},{7,6},{8,11},{9,8},{10,9... | collective-permute-start | bytes 1253384 | tf_op jit(solution)/shard_map/ppermute | solution.py:57
  187.9 17.6 %collective-permute-start.20 = (bf16[544,384]{1,0:T(8,128)(2,1)S(1)}, bf16[544,384]{1,0:T(8,128)(2,1)S(1)}, u32[]{:S(2)}, u32[]{:S(2)}) collective-permute-start(bf16[544,384]{1,0:T(8,128)(2,1)S(1)} %get-tuple-element.222), channel_id=1, source_target_pairs={{0,1},{1,2},{2,3},{3,0},{4,5},{5,6},{6,7},{7,4},{8,9},{9,10},{10,1... | collective-permute-start | bytes 1253384 | tf_op jit(solution)/shard_map/ppermute | solution.py:53
  189.4 17.8 %collective-permute-start.15 = (bf16[512,384]{1,0:T(8,128)(2,1)S(1)}, bf16[512,384]{1,0:T(8,128)(2,1)S(1)}, u32[]{:S(2)}, u32[]{:S(2)}) collective-permute-start(bf16[512,384]{1,0:T(8,128)(2,1)S(1)} %add_convert_fusion.3), channel_id=1, source_target_pairs={{0,4},{1,5},{2,6},{3,7},{4,0},{5,1},{6,2},{7,3},{8,12},{9,13},{10,... | collective-permute-start | bytes 1179656 | tf_op jit(solution)/shard_map/ppermute | solution.py:61
  193.6 38.4 %collective-permute-start.25 = (bf16[192,1536]{1,0:T(8,128)(2,1)S(1)}, bf16[192,1536]{1,0:T(8,128)(2,1)S(1)}, u32[]{:S(2)}, u32[]{:S(2)}) collective-permute-start(bf16[192,1536]{1,0:T(8,128)(2,1)S(1)} %get-tuple-element.219), channel_id=1, source_target_pairs={{0,32},{8,40},{16,48},{24,56},{32,64},{40,72},{48,80},{56,88},{64,... | collective-permute-start | bytes 1769480 | tf_op jit(solution)/shard_map/ppermute | solution.py:65
  194.7 37.4 %collective-permute-start.27 = (bf16[192,1536]{1,0:T(8,128)(2,1)S(1)}, bf16[192,1536]{1,0:T(8,128)(2,1)S(1)}, u32[]{:S(2)}, u32[]{:S(2)}) collective-permute-start(bf16[192,1536]{1,0:T(8,128)(2,1)S(1)} %get-tuple-element.221), channel_id=1, source_target_pairs={{0,96},{8,104},{16,112},{24,120},{32,0},{40,8},{48,16},{56,24},{64... | collective-permute-start | bytes 1769480 | tf_op jit(solution)/shard_map/ppermute | solution.py:69
  205.5 26.5 %collective-permute-start.30 = (bf16[192,1536]{1,0:T(8,128)(2,1)S(1)}, bf16[192,1536]{1,0:T(8,128)(2,1)S(1)}, u32[]{:S(2)}, u32[]{:S(2)}) collective-permute-start(bf16[192,1536]{1,0:T(8,128)(2,1)S(1)} %add_convert_fusion), channel_id=1, source_target_pairs={{0,16},{8,24},{16,0},{24,8},{32,48},{40,56},{48,32},{56,40},{64,80... | collective-permute-start | bytes 1769480 | tf_op jit(solution)/shard_map/ppermute | solution.py:73
  206.6 8.1 %collective-permute-start.19 = (bf16[544,384]{1,0:T(8,128)(2,1)S(1)}, bf16[544,384]{1,0:T(8,128)(2,1)S(1)}, u32[]{:S(2)}, u32[]{:S(2)}) collective-permute-start(bf16[544,384]{1,0:T(8,128)(2,1)S(1)} %get-tuple-element.225), channel_id=1, source_target_pairs={{0,3},{1,0},{2,1},{3,2},{4,7},{5,4},{6,5},{7,6},{8,11},{9,8},{10,9... | collective-permute-start | bytes 1253384 | tf_op jit(solution)/shard_map/ppermute | solution.py:57
  207.1 21.3 %collective-permute-start.22 = (bf16[544,384]{1,0:T(8,128)(2,1)S(1)}, bf16[544,384]{1,0:T(8,128)(2,1)S(1)}, u32[]{:S(2)}, u32[]{:S(2)}) collective-permute-start(bf16[544,384]{1,0:T(8,128)(2,1)S(1)} %add_convert_fusion.1), channel_id=1, source_target_pairs={{0,4},{1,5},{2,6},{3,7},{4,0},{5,1},{6,2},{7,3},{8,12},{9,13},{10,... | collective-permute-start | bytes 1253384 | tf_op jit(solution)/shard_map/ppermute | solution.py:61
  (33 other events, 365.0 us)
Sparse Core Ops, SparseCore 0:
  9.7 66.5 all-gather.1
